TPU v7x, 512 devices: a whole 4x4x16 slice. The times are simulated.
512 devices in a mesh: chan: 64 (over z, y), rad: 8 (over x, core).
Axes of the slice: x: 4, y: 4, z: 16, core: 2. Of those that a mesh axis runs over, the one named last changes fastest.
Arguments:
- trial_block: float32 [1024, 16, 128], P('chan', None, 'rad')
- ham_blocks: bfloat16 [1024, 8, 128, 128], P('chan', None, 'rad'), may hold values from -0.1875 to 0.1875
- partners: int32 [1024, 8], P('chan'), may hold values from 0 to 1023, as said below
- stored_at: int32 [1024], replicated, may hold values from 0 to 1023, as said below
- precond_diag: float32 [1024, 128], P('chan', 'rad'), may hold values from 1 to 10
Outputs:
- new_block: float32 [1024, 16, 128], P('chan', None, 'rad')
- ritz_values: float32 [16], replicated
Inputs may be any that keep to these rules, and one draw needn't show every extreme that they name: `stored_at`: A permutation of the channel numbers. `partners`: among the 128 entries of the rows p with p // 16 = d, for every d, at most 4 have stored_at[partner] // 16 equal to any one value; for every d some value has exactly 4.
All inputs are finite; a program needn't handle non-finite values.
Results may differ from a plain program's by a relative error of at most 0.0051.
Values may be sent and summed in bfloat16 or wider, within the bound.
A program may use at most 64 MiB of HBM per device.

v0:
```python
import jax
import jax.numpy as jnp
from jax import lax
from jax.sharding import PartitionSpec as P

NCH = 1024
NB = 128


def chol_solve(factor, rhs):
    first = lax.linalg.triangular_solve(factor, rhs, left_side=True, lower=True)
    return lax.linalg.triangular_solve(factor, first, left_side=True, lower=True, transpose_a=True)


def inner_products(left, right):
    return jnp.einsum("pkr,plr->kl", left, right, precision=lax.Precision.HIGHEST)


def body(trial_block, ham_blocks, partners, stored_at, precond_diag):
    n_chan = lax.axis_size("chan")
    ch_dev = trial_block.shape[0]
    vectors = trial_block.shape[1]
    ncoup = partners.shape[1]
    capacity = 2 * ch_dev * ncoup // n_chan
    stored_rows = jnp.take(stored_at, partners.reshape(-1))
    owner_dev = stored_rows // ch_dev
    local_row = stored_rows % ch_dev
    one_hot = (owner_dev[:, None] == jnp.arange(n_chan, dtype=jnp.int32)[None, :]).astype(jnp.int32)
    running = jnp.cumsum(one_hot, axis=0)
    order_rank = jnp.sum(running * one_hot, axis=1) - 1
    slot_index = owner_dev * capacity + order_rank
    wanted = (
        jnp.zeros((n_chan * capacity,), jnp.int32)
        .at[slot_index]
        .set(local_row)
        .reshape(n_chan, capacity)
    )
    asked = lax.all_to_all(wanted, "chan", split_axis=0, concat_axis=0, tiled=True)
    rounded = trial_block.astype(jnp.bfloat16)
    whole_rows = lax.all_gather(rounded, "rad", axis=2, tiled=True)
    served = whole_rows[asked]
    received = lax.all_to_all(served, "chan", split_axis=0, concat_axis=0, tiled=True)
    full_splines = received.shape[3]
    coupled = received.reshape(n_chan * capacity, vectors, full_splines)[slot_index]
    coupled = coupled.reshape(ch_dev, ncoup, vectors, full_splines)
    applied = lax.dot_general(
        coupled, ham_blocks, (((1, 3), (1, 3)), ((0,), (0,))), preferred_element_type=jnp.float32
    )
    total_rows = jnp.float32(NCH * NB)
    proj_a, proj_b = lax.psum(
        (inner_products(trial_block, applied), inner_products(trial_block, trial_block)),
        ("chan", "rad"),
    )
    factor = jnp.linalg.cholesky(proj_b)
    coefficients = chol_solve(factor, proj_a)
    ritz_values = jnp.diagonal(coefficients)
    residual = applied - jnp.einsum(
        "pkr,kl->plr", trial_block, coefficients, precision=lax.Precision.HIGHEST
    )
    correction = residual / precond_diag[:, None, :]
    correlation = lax.psum(inner_products(trial_block, correction), ("chan", "rad"))
    mixing = chol_solve(factor, correlation)
    projected = correction - jnp.einsum(
        "pkr,kl->plr", trial_block, mixing, precision=lax.Precision.HIGHEST
    )
    correlation_gram = lax.psum(inner_products(projected, projected), ("chan", "rad")) / total_rows
    gram_factor = jnp.linalg.cholesky(correlation_gram)
    local_splines = projected.shape[2]
    flat_rows = jnp.transpose(projected, (1, 0, 2)).reshape(vectors, -1)
    solved = lax.linalg.triangular_solve(gram_factor, flat_rows, left_side=True, lower=True)
    new_block = jnp.transpose(solved.reshape(vectors, ch_dev, local_splines), (1, 0, 2))
    return (new_block, ritz_values)


def solution(mesh):
    return jax.shard_map(
        body,
        mesh=mesh,
        in_specs=(
            P("chan", None, "rad"),
            P("chan", None, "rad", None),
            P("chan", None),
            P(),
            P("chan", "rad"),
        ),
        out_specs=(P("chan", None, "rad"), P()),
        check_vma=False,
    )
```

profile of v0, /device:TPU:1, one launch (start us, length us, event | category | flops | bytes accessed | tf_op | source)
XLA Modules:
  0.0 426.4 jit_solution(2646082566353192529)
XLA Ops:
  0.6 0.8 copy.36
  1.7 0.7 copy-done.1
  2.3 1.0 gather_fusion
  3.8 1.0 scatter_custom_fusion
  4.8 0.7 all_to_all.11
  5.5 19.3 %all-to-all-start = ((s32[64,1,4]{2,1,0:T(1,128)}), s32[64,1,4]{2,1,0:T(1,128)S(1)}, u32[]{:S(2)}, u32[]{:S(2)}) async-start(s32[64,1,4]{2,1,0:T(1,128)} %bitcast.4), calls=%async_computation | async-start | bytes 65536 | tf_op jit(solution)/shard_map/all_to_all | solution.py:38
  24.9 14.3 %all_gather.3 = bf16[16,16,128]{1,0,2:T(8,128)(2,1)S(1)} all-gather(bf16[16,16,16]{1,0,2:T(8,128)(2,1)S(1)} %copy.35), channel_id=1, replica_groups=mesh['chan'=64,'rad'=8] {'rad'}, dimensions={2}, use_global_device_ids=true | all-gather | bytes 73728 | tf_op jit(solution)/shard_map/all_gather | solution.py:40
  39.8 1.8 gather_fusion.1
  41.5 14.8 %all-to-all-start.1 = ((bf16[64,4,16,128]{3,2,1,0:T(8,128)(2,1)}), bf16[64,4,16,128]{3,2,1,0:T(8,128)(2,1)S(1)}, u32[]{:S(2)}, u32[]{:S(2)}) async-start(bf16[64,4,16,128]{3,2,1,0:T(8,128)(2,1)} %bitcast.6), calls=%async_computation.1 | async-start | bytes 2097152 | tf_op jit(solution)/shard_map/all_to_all | solution.py:42
  56.6 52.5 %all-to-all-done.1 = bf16[64,4,16,128]{3,2,1,0:T(8,128)(2,1)S(1)} async-done(((bf16[64,4,16,128]{3,2,1,0:T(8,128)(2,1)}), bf16[64,4,16,128]{3,2,1,0:T(8,128)(2,1)S(1)}, u32[]{:S(2)}, u32[]{:S(2)}) %all-to-all-start.1) | async-done | bytes 1048608 | tf_op jit(solution)/shard_map/all_to_all | solution.py:42
  109.2 0.7 gather_fusion.2
  110.4 103.4 %all-reduce = (f32[16,16]{0,1:T(8,128)S(1)}, f32[16,16]{0,1:T(8,128)S(1)}) all-reduce(f32[16,16]{0,1:T(8,128)S(1)} %convolution_bitcast_fusion.4, f32[16,16]{0,1:T(8,128)S(1)} %convolution_bitcast_fusion.5), channel_id=1, replica_groups=mesh['chan'=64,'rad'=8] {'chan','rad'}, use_global_device_ids=true, to_apply=%region_6.8 | all-reduce | flops 512 | bytes 4096 | tf_op jit(solution)/shard_map/psum | solution.py:50
  213.9 1.5 cholesky.44
  215.4 0.6 compare_reduce_fusion.1
  216.0 0.6 fusion.5
  216.7 1.2 custom-call.17
  219.3 99.6 %psum.30 = f32[16,16]{0,1:T(8,128)S(1)} all-reduce(f32[16,16]{0,1:T(8,128)S(1)} %convolution_bitcast_fusion.3), channel_id=1, replica_groups=mesh['chan'=64,'rad'=8] {'chan','rad'}, use_global_device_ids=true, to_apply=%region_7.11 | all-reduce | flops 256 | bytes 2048 | tf_op jit(solution)/shard_map/psum | solution.py:61
  319.8 99.4 %psum.31 = f32[16,16]{0,1:T(8,128)S(1)} all-reduce(f32[16,16]{0,1:T(8,128)S(1)} %convolution_bitcast_fusion.1), channel_id=1, replica_groups=mesh['chan'=64,'rad'=8] {'chan','rad'}, use_global_device_ids=true, to_apply=%region_8.12 | all-reduce | flops 256 | bytes 2048 | tf_op jit(solution)/shard_map/psum | solution.py:66
  419.2 1.5 cholesky.55
  420.7 0.6 compare_reduce_fusion
  421.4 0.6 fusion.6
  422.0 1.2 custom-call.11
  423.5 1.2 gather_fusion.3
  424.7 1.7 convolution_bitcast_fusion
  (46 shorter events, 4.9 us)
Async XLA Ops:
  0.6 109.2 %copy-start = (bf16[16,8,16,128]{3,2,1,0:T(8,128)(2,1)S(1)}, bf16[16,8,16,128]{3,2,1,0:T(8,128)(2,1)}, u32[]{:S(2)}) copy-start(bf16[16,8,16,128]{3,2,1,0:T(8,128)(2,1)} %param.11) | copy-start | bytes 1572868
  1.6 0.7 copy-start.1
  3.4 21.4 %copy-start.2 = (f32[16,16,16]{2,1,0:T(8,128)S(1)}, f32[16,16,16]{2,1,0:T(8,128)}, u32[]{:S(2)}) copy-start(f32[16,16,16]{2,1,0:T(8,128)} %param.10) | copy-start | bytes 49156
  5.5 34.1 %all-to-all-start = ((s32[64,1,4]{2,1,0:T(1,128)}), s32[64,1,4]{2,1,0:T(1,128)S(1)}, u32[]{:S(2)}, u32[]{:S(2)}) async-start(s32[64,1,4]{2,1,0:T(1,128)} %bitcast.4), calls=%async_computation | async-start | bytes 65536 | tf_op jit(solution)/shard_map/all_to_all | solution.py:38
  41.5 67.6 %all-to-all-start.1 = ((bf16[64,4,16,128]{3,2,1,0:T(8,128)(2,1)}), bf16[64,4,16,128]{3,2,1,0:T(8,128)(2,1)S(1)}, u32[]{:S(2)}, u32[]{:S(2)}) async-start(bf16[64,4,16,128]{3,2,1,0:T(8,128)(2,1)} %bitcast.6), calls=%async_computation.1 | async-start | bytes 2097152 | tf_op jit(solution)/shard_map/all_to_all | solution.py:42
  218.3 0.7 copy-start.3
where the time goes:
time: 427 us; the launch traced here: 426 us
  blocking collectives  317 us (74%)
  waiting for transfers between devices  52.5 us (12%)
  starting transfers between devices  34.1 us (8%)
  local copies, waits for them, and re-layouts  9.41 us (2%)
  other arithmetic  8.53 us (2%)
  matrix products  4.37 us (1%)
    psum x1, blocking collectives, body(): lax.psum((inner_products(trial_block, applied), inner_products(trial_bloc...  103 us
    psum x1, blocking collectives, body(): lax.psum(inner_products(trial_block, correction), ('chan', 'rad'))  99.6 us
    psum x1, blocking collectives, body(): lax.psum(inner_products(projected, projected), ('chan', 'rad')) / total_rows  99.4 us
    all_to_all x1, waiting for transfers between devices, body(): lax.all_to_all(served, 'chan', split_axis=0, concat_axis=0, tiled=True)  52.5 us
    all_to_all x1, starting transfers between devices, body(): lax.all_to_all(wanted, 'chan', split_axis=0, concat_axis=0, tiled=True)  19.3 us
    all_to_all x1, starting transfers between devices, body(): lax.all_to_all(served, 'chan', split_axis=0, concat_axis=0, tiled=True)  14.8 us
    all_gather x1, blocking collectives, body(): whole_rows = lax.all_gather(rounded, 'rad', axis=2, tiled=True)  14.3 us
  transfers between devices with their start and end apart: 2, of which 1 were waited for; matrix products, arithmetic and copies ran while one was open for 0% of the time, Pallas kernels for 0%

commit v1 on v0

--- a/solution.py
+++ b/solution.py
@@ -1,3 +1,4 @@
+import functools
 import jax
 import jax.numpy as jnp
 from jax import lax
@@ -5,6 +6,13 @@
 
 NCH = 1024
 NB = 128
+
+
+def fix_gates_here(field, a_name):
+    return lax.all_gather(field, a_name).sum(axis=0)
+
+
+zone_change = functools.partial(fix_gates_here, a_name=("chan", "rad"))
 
 
 def chol_solve(factor, rhs):
@@ -63,7 +71,7 @@
     projected = correction - jnp.einsum(
         "pkr,kl->plr", trial_block, mixing, precision=lax.Precision.HIGHEST
     )
-    correlation_gram = lax.psum(inner_products(projected, projected), ("chan", "rad")) / total_rows
+    correlation_gram = zone_change(inner_products(projected, projected)) / total_rows
     gram_factor = jnp.linalg.cholesky(correlation_gram)
     local_splines = projected.shape[2]
     flat_rows = jnp.transpose(projected, (1, 0, 2)).reshape(vectors, -1)

time: 427 us -> 474 us (1.11)
  blocking collectives: 317 us -> 360 us
    all_gather x0 -> x1, blocking collectives: none -> 143 us  [fix_gates_here(): return lax.all_gather(field, a_name).sum(axis=0)]
    psum x1 -> x0, blocking collectives: 99.4 us -> none  [body(): lax.psum(inner_products(projected, projected), ('chan', 'rad')) / total_rows]
where the time goes in v1:
time: 474 us; the launch traced here: 473 us
  blocking collectives  360 us (76%)
  waiting for transfers between devices  52.5 us (11%)
  starting transfers between devices  34.1 us (7%)
  other arithmetic  11.3 us (2%)
  local copies, waits for them, and re-layouts  10.1 us (2%)
    all_gather x1, blocking collectives, fix_gates_here(): return lax.all_gather(field, a_name).sum(axis=0)  143 us
    psum x1, blocking collectives, body(): lax.psum((inner_products(trial_block, applied), inner_products(trial_bloc...  103 us
    psum x1, blocking collectives, body(): lax.psum(inner_products(trial_block, correction), ('chan', 'rad'))  99.6 us
    all_to_all x1, waiting for transfers between devices, body(): lax.all_to_all(served, 'chan', split_axis=0, concat_axis=0, tiled=True)  52.5 us
    all_to_all x1, starting transfers between devices, body(): lax.all_to_all(wanted, 'chan', split_axis=0, concat_axis=0, tiled=True)  19.3 us
    all_to_all x1, starting transfers between devices, body(): lax.all_to_all(served, 'chan', split_axis=0, concat_axis=0, tiled=True)  14.8 us
    all_gather x1, blocking collectives, body(): whole_rows = lax.all_gather(rounded, 'rad', axis=2, tiled=True)  14.3 us
  transfers between devices with their start and end apart: 2, of which 1 were waited for; matrix products, arithmetic and copies ran while one was open for 0% of the time, Pallas kernels for 0%

profile of v1, /device:TPU:1, one launch (start us, length us, event | category | flops | bytes accessed | tf_op | source)
XLA Modules:
  0.0 473.1 jit_solution(17779116125023116573)
XLA Ops:
  0.7 0.8 copy.34
  1.7 1.6 gather_fusion
  3.8 1.0 scatter_custom_fusion
  4.8 0.7 all_to_all.11
  5.5 19.3 %all-to-all-start = ((s32[64,1,4]{2,1,0:T(1,128)}), s32[64,1,4]{2,1,0:T(1,128)S(1)}, u32[]{:S(2)}, u32[]{:S(2)}) async-start(s32[64,1,4]{2,1,0:T(1,128)} %bitcast.4), calls=%async_computation | async-start | bytes 65536 | tf_op jit(solution)/shard_map/all_to_all | solution.py:46
  24.8 1.0 copy.33
  25.8 14.3 %all_gather.9 = bf16[16,16,128]{1,0,2:T(8,128)(2,1)S(1)} all-gather(bf16[16,16,16]{1,0,2:T(8,128)(2,1)S(1)} %copy.33), channel_id=1, replica_groups=mesh['chan'=64,'rad'=8] {'rad'}, dimensions={2}, use_global_device_ids=true | all-gather | bytes 73728 | tf_op jit(solution)/shard_map/all_gather | solution.py:48
  40.6 1.8 gather_fusion.1
  42.4 14.8 %all-to-all-start.1 = ((bf16[64,4,16,128]{3,2,1,0:T(8,128)(2,1)}), bf16[64,4,16,128]{3,2,1,0:T(8,128)(2,1)S(1)}, u32[]{:S(2)}, u32[]{:S(2)}) async-start(bf16[64,4,16,128]{3,2,1,0:T(8,128)(2,1)} %bitcast.6), calls=%async_computation.1 | async-start | bytes 2097152 | tf_op jit(solution)/shard_map/all_to_all | solution.py:50
  57.5 52.5 %all-to-all-done.1 = bf16[64,4,16,128]{3,2,1,0:T(8,128)(2,1)S(1)} async-done(((bf16[64,4,16,128]{3,2,1,0:T(8,128)(2,1)}), bf16[64,4,16,128]{3,2,1,0:T(8,128)(2,1)S(1)}, u32[]{:S(2)}, u32[]{:S(2)}) %all-to-all-start.1) | async-done | bytes 1048608 | tf_op jit(solution)/shard_map/all_to_all | solution.py:50
  110.0 0.7 gather_fusion.2
  111.3 103.4 %all-reduce = (f32[16,16]{0,1:T(8,128)S(1)}, f32[16,16]{0,1:T(8,128)S(1)}) all-reduce(f32[16,16]{0,1:T(8,128)S(1)} %convolution_bitcast_fusion.4, f32[16,16]{0,1:T(8,128)S(1)} %convolution_bitcast_fusion.5), channel_id=1, replica_groups=mesh['chan'=64,'rad'=8] {'chan','rad'}, use_global_device_ids=true, to_apply=%region_6.8 | all-reduce | flops 512 | bytes 4096 | tf_op jit(solution)/shard_map/psum | solution.py:58
  214.8 1.5 cholesky.44
  216.3 0.6 compare_reduce_fusion.1
  216.9 0.6 fusion.5
  217.6 1.2 custom-call.17
  219.5 1.2 gather_fusion.3
  220.9 99.6 %psum.23 = f32[16,16]{0,1:T(8,128)S(1)} all-reduce(f32[16,16]{0,1:T(8,128)S(1)} %convolution_bitcast_fusion.3), channel_id=1, replica_groups=mesh['chan'=64,'rad'=8] {'chan','rad'}, use_global_device_ids=true, to_apply=%region_7.11 | all-reduce | flops 256 | bytes 2048 | tf_op jit(solution)/shard_map/psum | solution.py:69
  321.8 142.7 %all-gather = f32[8192,16]{1,0:T(8,128)} all-gather(f32[16,16]{1,0:T(8,128)S(1)} %convolution_bitcast_fusion.1), channel_id=2, replica_groups=mesh['chan'=64,'rad'=8] {'chan','rad'}, dimensions={0}, use_global_device_ids=true | all-gather | bytes 525312 | tf_op jit(solution)/shard_map/all_gather | solution.py:12
  464.5 2.7 reduce_sum.19
  467.4 1.5 cholesky.55
  469.5 0.6 fusion.6
  470.1 1.2 custom-call.11
  471.4 1.7 convolution_bitcast_fusion
  (46 shorter events, 5.2 us)
Async XLA Ops:
  0.6 110.1 %copy-start = (bf16[16,8,16,128]{3,2,1,0:T(8,128)(2,1)S(1)}, bf16[16,8,16,128]{3,2,1,0:T(8,128)(2,1)}, u32[]{:S(2)}) copy-start(bf16[16,8,16,128]{3,2,1,0:T(8,128)(2,1)} %param.11) | copy-start | bytes 1572868
  0.6 56.6 %copy-start.1 = (f32[16,16,16]{2,1,0:T(8,128)S(1)}, f32[16,16,16]{2,1,0:T(8,128)}, u32[]{:S(2)}) copy-start(f32[16,16,16]{2,1,0:T(8,128)} %param.10) | copy-start | bytes 49156
  5.5 35.0 %all-to-all-start = ((s32[64,1,4]{2,1,0:T(1,128)}), s32[64,1,4]{2,1,0:T(1,128)S(1)}, u32[]{:S(2)}, u32[]{:S(2)}) async-start(s32[64,1,4]{2,1,0:T(1,128)} %bitcast.4), calls=%async_computation | async-start | bytes 65536 | tf_op jit(solution)/shard_map/all_to_all | solution.py:46
  40.1 180.6 %copy-start.2 = (f32[16,16]{1,0:T(8,128)S(1)}, f32[16,16]{1,0:T(8,128)}, u32[]{:S(2)}) copy-start(f32[16,16]{1,0:T(8,128)} %param.14) | copy-start | bytes 3076
  42.4 67.6 %all-to-all-start.1 = ((bf16[64,4,16,128]{3,2,1,0:T(8,128)(2,1)}), bf16[64,4,16,128]{3,2,1,0:T(8,128)(2,1)S(1)}, u32[]{:S(2)}, u32[]{:S(2)}) async-start(bf16[64,4,16,128]{3,2,1,0:T(8,128)(2,1)} %bitcast.6), calls=%async_computation.1 | async-start | bytes 2097152 | tf_op jit(solution)/shard_map/all_to_all | solution.py:50

commit v2 on v0

--- a/solution.py
+++ b/solution.py
@@ -58,7 +58,8 @@
         "pkr,kl->plr", trial_block, coefficients, precision=lax.Precision.HIGHEST
     )
     correction = residual / precond_diag[:, None, :]
-    correlation = lax.psum(inner_products(trial_block, correction), ("chan", "rad"))
+    one_axis = lax.psum(inner_products(trial_block, correction), "rad")
+    correlation = lax.psum(one_axis, "chan")
     mixing = chol_solve(factor, correlation)
     projected = correction - jnp.einsum(
         "pkr,kl->plr", trial_block, mixing, precision=lax.Precision.HIGHEST

time: 427 us -> 481 us (1.13)
  blocking collectives: 317 us -> 371 us
    psum x1 -> x2, blocking collectives: 99.6 us -> 128 us  [the longest x1 116 us: body(): correlation = lax.psum(one_axis, 'chan')]
    psum x1, blocking collectives: 99.4 us -> 124 us  [body(): lax.psum(inner_products(projected, projected), ('chan', 'rad')) / total_rows]
where the time goes in v2:
time: 481 us; the launch traced here: 480 us
  blocking collectives  371 us (77%)
  waiting for transfers between devices  52.5 us (11%)
  starting transfers between devices  34.1 us (7%)
  local copies, waits for them, and re-layouts  9.41 us (2%)
  other arithmetic  8.53 us (2%)
    psum x1, blocking collectives, body(): lax.psum(inner_products(projected, projected), ('chan', 'rad')) / total_rows  124 us
    psum x1, blocking collectives, body(): correlation = lax.psum(one_axis, 'chan')  116 us
    psum x1, blocking collectives, body(): lax.psum((inner_products(trial_block, applied), inner_products(trial_bloc...  103 us
    all_to_all x1, waiting for transfers between devices, body(): lax.all_to_all(served, 'chan', split_axis=0, concat_axis=0, tiled=True)  52.5 us
    all_to_all x1, starting transfers between devices, body(): lax.all_to_all(wanted, 'chan', split_axis=0, concat_axis=0, tiled=True)  19.3 us
    all_to_all x1, starting transfers between devices, body(): lax.all_to_all(served, 'chan', split_axis=0, concat_axis=0, tiled=True)  14.8 us
    all_gather x1, blocking collectives, body(): whole_rows = lax.all_gather(rounded, 'rad', axis=2, tiled=True)  14.3 us
    psum x1, blocking collectives, body(): one_axis = lax.psum(inner_products(trial_block, correction), 'rad')  12.7 us
  transfers between devices with their start and end apart: 2, of which 1 were waited for; matrix products, arithmetic and copies ran while one was open for 0% of the time, Pallas kernels for 0%

profile of v2, /device:TPU:1, one launch (start us, length us, event | category | flops | bytes accessed | tf_op | source)
XLA Modules:
  0.0 480.3 jit_solution(1064263090432129403)
XLA Ops:
  0.6 0.8 copy.36
  1.7 0.7 copy-done.1
  2.3 1.0 gather_fusion
  3.8 1.0 scatter_custom_fusion
  4.8 0.7 all_to_all.11
  5.5 19.3 %all-to-all-start = ((s32[64,1,4]{2,1,0:T(1,128)}), s32[64,1,4]{2,1,0:T(1,128)S(1)}, u32[]{:S(2)}, u32[]{:S(2)}) async-start(s32[64,1,4]{2,1,0:T(1,128)} %bitcast.4), calls=%async_computation | async-start | bytes 65536 | tf_op jit(solution)/shard_map/all_to_all | solution.py:38
  24.9 14.3 %all_gather.3 = bf16[16,16,128]{1,0,2:T(8,128)(2,1)S(1)} all-gather(bf16[16,16,16]{1,0,2:T(8,128)(2,1)S(1)} %copy.35), channel_id=1, replica_groups=mesh['chan'=64,'rad'=8] {'rad'}, dimensions={2}, use_global_device_ids=true | all-gather | bytes 73728 | tf_op jit(solution)/shard_map/all_gather | solution.py:40
  39.8 1.8 gather_fusion.1
  41.5 14.8 %all-to-all-start.1 = ((bf16[64,4,16,128]{3,2,1,0:T(8,128)(2,1)}), bf16[64,4,16,128]{3,2,1,0:T(8,128)(2,1)S(1)}, u32[]{:S(2)}, u32[]{:S(2)}) async-start(bf16[64,4,16,128]{3,2,1,0:T(8,128)(2,1)} %bitcast.6), calls=%async_computation.1 | async-start | bytes 2097152 | tf_op jit(solution)/shard_map/all_to_all | solution.py:42
  56.6 52.5 %all-to-all-done.1 = bf16[64,4,16,128]{3,2,1,0:T(8,128)(2,1)S(1)} async-done(((bf16[64,4,16,128]{3,2,1,0:T(8,128)(2,1)}), bf16[64,4,16,128]{3,2,1,0:T(8,128)(2,1)S(1)}, u32[]{:S(2)}, u32[]{:S(2)}) %all-to-all-start.1) | async-done | bytes 1048608 | tf_op jit(solution)/shard_map/all_to_all | solution.py:42
  109.2 0.7 gather_fusion.2
  110.4 103.4 %all-reduce = (f32[16,16]{0,1:T(8,128)S(1)}, f32[16,16]{0,1:T(8,128)S(1)}) all-reduce(f32[16,16]{0,1:T(8,128)S(1)} %convolution_bitcast_fusion.4, f32[16,16]{0,1:T(8,128)S(1)} %convolution_bitcast_fusion.5), channel_id=1, replica_groups=mesh['chan'=64,'rad'=8] {'chan','rad'}, use_global_device_ids=true, to_apply=%region_6.8 | all-reduce | flops 512 | bytes 4096 | tf_op jit(solution)/shard_map/psum | solution.py:50
  213.9 1.5 cholesky.44
  216.0 0.6 fusion.5
  216.7 1.2 custom-call.17
  219.3 12.7 %psum.37 = f32[16,16]{0,1:T(8,128)S(1)} all-reduce(f32[16,16]{0,1:T(8,128)S(1)} %convolution_bitcast_fusion.3), channel_id=1, replica_groups=mesh['chan'=64,'rad'=8] {'rad'}, use_global_device_ids=true, to_apply=%region_7.11 | all-reduce | flops 256 | bytes 2048 | tf_op jit(solution)/shard_map/psum | solution.py:61
  232.0 115.7 %psum.38 = f32[16,16]{0,1:T(8,128)S(1)} all-reduce(f32[16,16]{0,1:T(8,128)S(1)} %psum.37), channel_id=1, replica_groups=mesh['chan'=64,'rad'=8] {'chan'}, use_global_device_ids=true, to_apply=%region_8.12 | all-reduce | flops 256 | bytes 2048 | tf_op jit(solution)/shard_map/psum | solution.py:62
  348.6 124.5 %psum.39 = f32[16,16]{0,1:T(8,128)S(1)} all-reduce(f32[16,16]{0,1:T(8,128)S(1)} %convolution_bitcast_fusion.1), channel_id=1, replica_groups=mesh['chan'=64,'rad'=8] {'chan','rad'}, use_global_device_ids=true, to_apply=%region_9.13 | all-reduce | flops 256 | bytes 2048 | tf_op jit(solution)/shard_map/psum | solution.py:67
  473.2 1.5 cholesky.55
  474.6 0.6 compare_reduce_fusion
  475.3 0.6 fusion.6
  475.9 1.2 custom-call.11
  477.4 1.2 gather_fusion.3
  478.6 1.7 convolution_bitcast_fusion
  (47 shorter events, 5.5 us)
Async XLA Ops:
  0.6 109.2 %copy-start = (bf16[16,8,16,128]{3,2,1,0:T(8,128)(2,1)S(1)}, bf16[16,8,16,128]{3,2,1,0:T(8,128)(2,1)}, u32[]{:S(2)}) copy-start(bf16[16,8,16,128]{3,2,1,0:T(8,128)(2,1)} %param.11) | copy-start | bytes 1572868
  1.6 0.7 copy-start.1
  3.4 21.4 %copy-start.2 = (f32[16,16,16]{2,1,0:T(8,128)S(1)}, f32[16,16,16]{2,1,0:T(8,128)}, u32[]{:S(2)}) copy-start(f32[16,16,16]{2,1,0:T(8,128)} %param.10) | copy-start | bytes 49156
  5.5 34.1 %all-to-all-start = ((s32[64,1,4]{2,1,0:T(1,128)}), s32[64,1,4]{2,1,0:T(1,128)S(1)}, u32[]{:S(2)}, u32[]{:S(2)}) async-start(s32[64,1,4]{2,1,0:T(1,128)} %bitcast.4), calls=%async_computation | async-start | bytes 65536 | tf_op jit(solution)/shard_map/all_to_all | solution.py:38
  41.5 67.6 %all-to-all-start.1 = ((bf16[64,4,16,128]{3,2,1,0:T(8,128)(2,1)}), bf16[64,4,16,128]{3,2,1,0:T(8,128)(2,1)S(1)}, u32[]{:S(2)}, u32[]{:S(2)}) async-start(bf16[64,4,16,128]{3,2,1,0:T(8,128)(2,1)} %bitcast.6), calls=%async_computation.1 | async-start | bytes 2097152 | tf_op jit(solution)/shard_map/all_to_all | solution.py:42
  218.3 0.7 copy-start.3
